TPU v7x, 256 devices: a whole 4x4x8 slice. The times are simulated.
256 devices in a mesh: ctx: 8 (over x, z_hi), serve: 32 (over z_lo, y, core).
Axes of the slice: x: 4, y: 4, z: 8 (z_hi: 2, z_lo: 4; z = z_hi * 4 + z_lo), core: 2. Of those that a mesh axis runs over, the one named last changes fastest.
Arguments:
- queries: bfloat16 [8192, 8192], P(('ctx', 'serve')), may hold values from -6 to 6
- key_rows: bfloat16 [8192, 1024], P(('ctx', 'serve')), may hold values from -6 to 6
- value_rows: bfloat16 [8192, 1024], P(('ctx', 'serve')), may hold values from -6 to 6
- page_owner: int32 [512], P('ctx'), may hold values from 0 to 31, as said below
- page_slot: int32 [512], P('ctx'), may hold values from 0 to 3, as said below
Outputs:
- attended: bfloat16 [8192, 8192], P(('ctx', 'serve'))
- key_cache: bfloat16 [1024, 16, 1024], P(('ctx', 'serve'))
- value_cache: bfloat16 [1024, 16, 1024], P(('ctx', 'serve'))
Inputs may be any that keep to these rules, and one draw needn't show every extreme that they name: `page_owner`: within each block of 64 consecutive pages some owner receives exactly 4 pages and no owner more. `page_slot`: within each block of 64 consecutive pages no owner receives two pages in one slot.
All inputs are finite; a program needn't handle non-finite values.
Results may differ from a plain program's by a relative error of at most 0.0065.
Values may be sent and summed in bfloat16 or wider, within the bound.
A program may use at most 64 MiB of HBM per device.

v0:
```python
import math

import jax
import jax.numpy as jnp
from jax import lax
from jax.sharding import PartitionSpec as P

HEAD_DIM = 128
PAGE = 16


def gather_pages(key_rows, value_rows):
    return (
        lax.all_gather(key_rows, "serve", axis=0, tiled=True),
        lax.all_gather(value_rows, "serve", axis=0, tiled=True),
    )


def token_positions(first_row, row_count):
    global_rows = first_row + jnp.arange(row_count, dtype=jnp.int32)
    return global_rows


def attend(running, query_block, key_block, value_block, key_pos, query_pos):

    def compute(current):
        run_max, run_sum, run_acc = current
        scores = jnp.einsum(
            "thd,kd->thk", query_block, key_block, preferred_element_type=jnp.float32
        )
        scores = scores * (1.0 / math.sqrt(key_block.shape[1]))
        causal = (key_pos[None, :] <= query_pos[:, None])[:, None, :]
        block_max = jnp.max(jnp.where(causal, scores, -1e30), axis=-1)
        new_max = jnp.maximum(run_max, block_max)
        expo = jnp.where(causal, jnp.exp(scores - new_max[..., None]), 0.0)
        rescale = jnp.exp(run_max - new_max)
        new_sum = run_sum * rescale + jnp.sum(expo, axis=-1)
        product = jnp.einsum(
            "thk,kd->thd",
            expo.astype(jnp.bfloat16),
            value_block,
            preferred_element_type=jnp.float32,
        )
        new_acc = run_acc * rescale[..., None] + product
        return (new_max, new_sum, new_acc)

    def unchanged(current):
        return current

    return lax.cond(jnp.min(key_pos) > jnp.max(query_pos), unchanged, compute, running)


def shards(queries, key_rows, value_rows, page_owner, page_slot):
    n_serve = lax.axis_size("serve")
    serve_here = lax.axis_index("serve")
    ctx_here = lax.axis_index("ctx")
    row_count = key_rows.shape[0]
    kv_heads = key_rows.shape[1] // HEAD_DIM
    copies = n_serve // kv_heads
    query_local = lax.all_to_all(queries, "serve", split_axis=1, concat_axis=0, tiled=True)
    tok_dev = query_local.shape[0]
    q_heads = query_local.shape[1] // HEAD_DIM
    key_copies = jnp.repeat(
        key_rows.reshape(row_count, kv_heads, HEAD_DIM), copies, axis=1
    ).reshape(row_count, n_serve * HEAD_DIM)
    value_copies = jnp.repeat(
        value_rows.reshape(row_count, kv_heads, HEAD_DIM), copies, axis=1
    ).reshape(row_count, n_serve * HEAD_DIM)
    key_own, value_own = (
        lax.all_to_all(key_copies, "serve", split_axis=1, concat_axis=0, tiled=True),
        lax.all_to_all(value_copies, "serve", split_axis=1, concat_axis=0, tiled=True),
    )
    query_block = query_local.reshape(tok_dev, q_heads, HEAD_DIM)
    query_pos = token_positions(ctx_here * tok_dev, tok_dev)
    start_state = (
        jnp.full((tok_dev, q_heads), -1e30, jnp.float32),
        jnp.zeros((tok_dev, q_heads), jnp.float32),
        jnp.zeros((tok_dev, q_heads, HEAD_DIM), jnp.float32),
    )
    key_piece = lax.all_gather(key_own, "ctx", axis=0, tiled=True)
    value_piece = lax.all_gather(value_own, "ctx", axis=0, tiled=True)
    piece_rows = key_piece.shape[0]
    key_pos = token_positions(jnp.int32(0), piece_rows)
    running = start_state
    piece_rows = key_piece.shape[0]
    block_count = piece_rows // 1024

    def scan_step(current, blocks_in):
        key_block, value_block, pos_block = blocks_in
        return (attend(current, query_block, key_block, value_block, pos_block, query_pos), None)

    running, unused = lax.scan(
        scan_step,
        running,
        (
            key_piece.reshape(block_count, 1024, HEAD_DIM),
            value_piece.reshape(block_count, 1024, HEAD_DIM),
            key_pos.reshape(block_count, 1024),
        ),
    )
    run_max, run_sum, run_acc = running
    result = (
        (run_acc / run_sum[..., None]).astype(jnp.bfloat16).reshape(tok_dev, q_heads * HEAD_DIM)
    )
    attended = lax.all_to_all(result, "serve", split_axis=0, concat_axis=1, tiled=True)
    key_all, value_all = gather_pages(key_rows, value_rows)
    per_block = page_owner.shape[0]
    slot_count = 2 * per_block // n_serve
    kv_width = key_all.shape[1]
    page_index = jnp.arange(per_block, dtype=jnp.int32)
    slot_index = jnp.arange(slot_count, dtype=jnp.int32)
    matched = (page_owner[None, :] == serve_here) & (page_slot[None, :] == slot_index[:, None])
    chosen = jnp.sum(jnp.where(matched, page_index[None, :], 0), axis=1)
    filled = jnp.any(matched, axis=1)
    key_pages = key_all.reshape(per_block, PAGE, kv_width)
    value_pages = value_all.reshape(per_block, PAGE, kv_width)
    key_cache = jnp.where(
        filled[:, None, None], jnp.take(key_pages, chosen, axis=0), jnp.zeros((), jnp.bfloat16)
    )
    value_cache = jnp.where(
        filled[:, None, None], jnp.take(value_pages, chosen, axis=0), jnp.zeros((), jnp.bfloat16)
    )
    return (attended, key_cache, value_cache)


def solution(mesh):
    placed = (
        P(("ctx", "serve"), None),
        P(("ctx", "serve"), None),
        P(("ctx", "serve"), None),
        P("ctx"),
        P("ctx"),
    )
    return jax.shard_map(
        shards,
        mesh=mesh,
        in_specs=placed,
        out_specs=(
            P(("ctx", "serve"), None),
            P(("ctx", "serve"), None, None),
            P(("ctx", "serve"), None, None),
        ),
        check_vma=False,
    )
```

profile of v0, /device:TPU:2, one launch (start us, length us, event | category | flops | bytes accessed | tf_op | source)
XLA Modules:
  0.0 306.0 jit_solution(13427952339213813426)
XLA Ops:
  8.1 19.9 %all_to_all.73 = bf16[32,32,128]{2,0,1:T(8,128)(2,1)} all-to-all(bf16[32,32,128]{2,0,1:T(8,128)(2,1)S(1)} %bitcast.60), channel_id=1, replica_groups=mesh['ctx'=8,'serve'=32] {'serve'}, dimensions={1} | all-to-all | bytes 524288 | tf_op jit(solution)/shard_map/all_to_all | solution.py:70
  29.0 14.8 %all_to_all.74 = bf16[32,32,128]{2,0,1:T(8,128)(2,1)} all-to-all(bf16[32,32,128]{2,0,1:T(8,128)(2,1)S(1)} %bitcast.61), channel_id=1, replica_groups=mesh['ctx'=8,'serve'=32] {'serve'}, dimensions={1} | all-to-all | bytes 524288 | tf_op jit(solution)/shard_map/all_to_all | solution.py:71
  47.1 3.9 %all-to-all-start.1 = ((bf16[32,32,256]{2,0,1:T(8,128)(2,1)}), bf16[32,32,256]{2,0,1:T(8,128)(2,1)S(1)}, u32[]{:S(2)}, u32[]{:S(2)}) async-start(bf16[32,32,256]{2,0,1:T(8,128)(2,1)} %bitcast.57), calls=%async_computation.1 | async-start | bytes 1048576 | tf_op jit(solution)/shard_map/all_to_all | solution.py:60
  52.4 14.5 %all-to-all-done.1 = bf16[32,32,256]{2,0,1:T(8,128)(2,1)S(1)} async-done(((bf16[32,32,256]{2,0,1:T(8,128)(2,1)}), bf16[32,32,256]{2,0,1:T(8,128)(2,1)S(1)}, u32[]{:S(2)}, u32[]{:S(2)}) %all-to-all-start.1) | async-done | bytes 524320 | tf_op jit(solution)/shard_map/all_to_all | solution.py:60
  67.1 35.4 %all-gather.5.cloned.1.call-done = bf16[8192,128]{1,0:T(8,128)(2,1)} async-done(((bf16[1024,128]{1,0:T(8,128)(2,1)}), bf16[8192,128]{1,0:T(8,128)(2,1)}) %all-gather.5.cloned.1.call-update) | async-done | bytes 2097168 | tf_op jit(solution)/shard_map/all_gather | solution.py:80
  102.4 74.4 %all-gather.7.cloned.1.call-done = bf16[8192,128]{1,0:T(8,128)(2,1)} async-done(((bf16[1024,128]{1,0:T(8,128)(2,1)}), bf16[8192,128]{1,0:T(8,128)(2,1)}) %all-gather.7.cloned.1.call-update) | async-done | bytes 2097168 | tf_op jit(solution)/shard_map/all_gather | solution.py:81
  176.9 44.6 %while.16 = (s32[]{:T(128)}, f32[1024,2]{0,1:T(2,128)S(1)}, f32[1024,2]{0,1:T(2,128)S(1)}, f32[1024,2,128]{2,0,1:T(8,128)S(1)}, s32[8,1024]{1,0:T(8,128)S(1)}, /...) while((s32[]{:T(128)}, f32[1024,2]{0,1:T(2,128)S(1)}, ...), condition=%wide.region_7.8_spmd.clone, body=%wide.region_1.7_spmd.clone.sunk | while | flops 1098389504 | bytes 32666896 | solution.py:92
  179.0 9.2 %conditional.3 = (f32[1024,2]{0,1:T(2,128)S(1)}, f32[1024,2]{0,1:T(2,128)S(1)}, f32[1024,2,128]{2,0,1:T(8,128)S(1)}) conditional(s32[]{:T(128)} %convert_element_type.20, (s32[1,1024]{1,0:T(1,128)S(1)}, s32[]{:T(128)}, bf16[8,1024,128]{2,1,0:T(8,128)(2,1)}, s32[]{:T(128)}, bf16[1024,2,128]{2,0,1:T(8,128)(2,1)S(1)}, ...), branch_computations={%region_3.5_spmd, %region_6.6_spmd} | conditional | flops 1098388480 | bytes 32637980 | solution.py:50
  179.7 2.8 fusion.2
  182.5 2.0 fusion.6
  184.5 3.7 %fusion.10 = f32[1024,2,128]{2,0,1:T(8,128)S(1)} fusion(f32[1024,1024,2]{1,0,2:T(8,128)S(1)} %get-tuple-element.263, f32[1024,2]{0,1:T(2,128)S(1)} %max.4, pred[1024,1024]{0,1:T(8,128)(4,1)S(1)} %broadcast_compare_fusion, f32[1024,2,128]{2,0,1:T(8,128)S(1)} %get-tuple-element.156, f32[1024,2]{0,1:T(2,128)S(1)} %get-tuple-element.259, ...), kind=kOutput, calls=%fused_computation.13 | convolution fusion | flops 545783808 | bytes 11813376 | tf_op jit(solution)/shard_map/while/body/eval_jaxpr/cond/branch_0_fun/thk,kd->thd/dot_general | solution.py:38
  190.3 9.2 %conditional.3 = (f32[1024,2]{0,1:T(2,128)S(1)}, f32[1024,2]{0,1:T(2,128)S(1)}, f32[1024,2,128]{2,0,1:T(8,128)S(1)}) conditional(s32[]{:T(128)} %convert_element_type.20, (s32[1,1024]{1,0:T(1,128)S(1)}, s32[]{:T(128)}, bf16[8,1024,128]{2,1,0:T(8,128)(2,1)}, s32[]{:T(128)}, bf16[1024,2,128]{2,0,1:T(8,128)(2,1)S(1)}, ...), branch_computations={%region_3.5_spmd, %region_6.6_spmd} | conditional | flops 1098388480 | bytes 32637980 | solution.py:50
  191.0 2.8 fusion.2
  193.8 2.0 fusion.6
  195.8 3.7 %fusion.10 = f32[1024,2,128]{2,0,1:T(8,128)S(1)} fusion(f32[1024,1024,2]{1,0,2:T(8,128)S(1)} %get-tuple-element.263, f32[1024,2]{0,1:T(2,128)S(1)} %max.4, pred[1024,1024]{0,1:T(8,128)(4,1)S(1)} %broadcast_compare_fusion, f32[1024,2,128]{2,0,1:T(8,128)S(1)} %get-tuple-element.156, f32[1024,2]{0,1:T(2,128)S(1)} %get-tuple-element.259, ...), kind=kOutput, calls=%fused_computation.13 | convolution fusion | flops 545783808 | bytes 11813376 | tf_op jit(solution)/shard_map/while/body/eval_jaxpr/cond/branch_0_fun/thk,kd->thd/dot_general | solution.py:38
  201.6 9.2 %conditional.3 = (f32[1024,2]{0,1:T(2,128)S(1)}, f32[1024,2]{0,1:T(2,128)S(1)}, f32[1024,2,128]{2,0,1:T(8,128)S(1)}) conditional(s32[]{:T(128)} %convert_element_type.20, (s32[1,1024]{1,0:T(1,128)S(1)}, s32[]{:T(128)}, bf16[8,1024,128]{2,1,0:T(8,128)(2,1)}, s32[]{:T(128)}, bf16[1024,2,128]{2,0,1:T(8,128)(2,1)S(1)}, ...), branch_computations={%region_3.5_spmd, %region_6.6_spmd} | conditional | flops 1098388480 | bytes 32637980 | solution.py:50
  202.3 2.8 fusion.2
  205.1 2.0 fusion.6
  207.1 3.7 %fusion.10 = f32[1024,2,128]{2,0,1:T(8,128)S(1)} fusion(f32[1024,1024,2]{1,0,2:T(8,128)S(1)} %get-tuple-element.263, f32[1024,2]{0,1:T(2,128)S(1)} %max.4, pred[1024,1024]{0,1:T(8,128)(4,1)S(1)} %broadcast_compare_fusion, f32[1024,2,128]{2,0,1:T(8,128)S(1)} %get-tuple-element.156, f32[1024,2]{0,1:T(2,128)S(1)} %get-tuple-element.259, ...), kind=kOutput, calls=%fused_computation.13 | convolution fusion | flops 545783808 | bytes 11813376 | tf_op jit(solution)/shard_map/while/body/eval_jaxpr/cond/branch_0_fun/thk,kd->thd/dot_general | solution.py:38
  223.6 4.7 %all-to-all-start.3 = ((bf16[32,32,256]{2,1,0:T(8,128)(2,1)}), bf16[32,32,256]{2,1,0:T(8,128)(2,1)S(1)}, u32[]{:S(2)}, u32[]{:S(2)}) async-start(bf16[32,32,256]{2,1,0:T(8,128)(2,1)} %all_to_all.65), calls=%async_computation.3 | async-start | bytes 1048576 | tf_op jit(solution)/shard_map/all_to_all | solution.py:105
  228.5 7.2 %all-gather.11.cloned.1.call-done = bf16[1024,1024]{1,0:T(8,128)(2,1)} async-done(((bf16[32,1024]{1,0:T(8,128)(2,1)}), bf16[1024,1024]{1,0:T(8,128)(2,1)}) %all-gather.11.cloned.1.call-update) | async-done | bytes 2097168 | tf_op jit(solution)/shard_map/all_gather | solution.py:15
  235.7 2.1 gather_fusion.1
  237.9 57.9 %all-gather.9.cloned.1.call-done = bf16[1024,1024]{1,0:T(8,128)(2,1)} async-done(((bf16[32,1024]{1,0:T(8,128)(2,1)}), bf16[1024,1024]{1,0:T(8,128)(2,1)}) %all-gather.9.cloned.1.call-update) | async-done | bytes 2097168 | tf_op jit(solution)/shard_map/all_gather | solution.py:14
  295.7 2.1 gather_fusion
  (80 shorter events, 18.6 us)
Async XLA Ops:
  7.2 95.3 %all-gather.5.cloned.1.call-start = ((), (), s32[]{:S(2)}) async-start(), calls=%async_computation.4 | async-start | bytes 2359296 | tf_op jit(solution)/shard_map/all_gather | solution.py:80
  28.1 148.8 %all-gather.7.cloned.1.call-start = ((), (), s32[]{:S(2)}) async-start(), calls=%async_computation.5 | async-start | bytes 2359296 | tf_op jit(solution)/shard_map/all_gather | solution.py:81
  43.9 191.8 %all-gather.11.cloned.1.call-start = ((), (), s32[]{:S(2)}) async-start(), calls=%async_computation.7 | async-start | bytes 2162688 | tf_op jit(solution)/shard_map/all_gather | solution.py:15
  44.6 251.1 %all-gather.9.cloned.1.call-start = ((), (), s32[]{:S(2)}) async-start(), calls=%async_computation.6 | async-start | bytes 2162688 | tf_op jit(solution)/shard_map/all_gather | solution.py:14
  47.1 19.8 %all-to-all-start.1 = ((bf16[32,32,256]{2,0,1:T(8,128)(2,1)}), bf16[32,32,256]{2,0,1:T(8,128)(2,1)S(1)}, u32[]{:S(2)}, u32[]{:S(2)}) async-start(bf16[32,32,256]{2,0,1:T(8,128)(2,1)} %bitcast.57), calls=%async_computation.1 | async-start | bytes 1048576 | tf_op jit(solution)/shard_map/all_to_all | solution.py:60
  176.9 51.3 %copy-start = (s32[64]{0:T(128)S(1)}, s32[64]{0:T(128)}, u32[]{:S(2)}) copy-start(s32[64]{0:T(128)} %param.15) | copy-start | bytes 772
  223.6 75.1 %all-to-all-start.3 = ((bf16[32,32,256]{2,1,0:T(8,128)(2,1)}), bf16[32,32,256]{2,1,0:T(8,128)(2,1)S(1)}, u32[]{:S(2)}, u32[]{:S(2)}) async-start(bf16[32,32,256]{2,1,0:T(8,128)(2,1)} %all_to_all.65), calls=%async_computation.3 | async-start | bytes 1048576 | tf_op jit(solution)/shard_map/all_to_all | solution.py:105
Sparse Core Ops, SparseCore 0:
  28.2 74.2 all-gather.4
  105.0 71.7 all-gather.6
  178.7 56.9 all-gather.10
  237.4 58.2 all-gather.8
where the time goes:
time: 311 us; the launch traced here: 306 us
  waiting for transfers between devices  191 us (61%)
  blocking collectives  34.8 us (11%)
  matrix products  19.3 us (6%)
  other arithmetic  16.5 us (5%)
  between operations  13.9 us (4%)
  loops' own time  11.6 us (4%)
  local copies, waits for them, and re-layouts  10.8 us (3%)
  starting transfers between devices  8.73 us (3%)
    all_gather x1, waiting for transfers between devices, shards(): value_piece = lax.all_gather(value_own, 'ctx', axis=0, tiled=True)  74.4 us
    all_gather x1, waiting for transfers between devices, gather_pages(): lax.all_gather(key_rows, 'serve', axis=0, tiled=True)  57.9 us
    all_gather x1, waiting for transfers between devices, shards(): key_piece = lax.all_gather(key_own, 'ctx', axis=0, tiled=True)  35.4 us
    all_to_all x1, blocking collectives, shards(): lax.all_to_all(key_copies, 'serve', split_axis=1, concat_axis=0, tiled=True)  19.9 us
    all_to_all x1, blocking collectives, shards(): lax.all_to_all(value_copies, 'serve', split_axis=1, concat_axis=0, tiled=...  14.8 us
    all_to_all x1, waiting for transfers between devices, shards(): lax.all_to_all(queries, 'serve', split_axis=1, concat_axis=0, tiled=True)  14.5 us
    another operation x1, loops' own time, shards(): lax.scan(scan_step, running, (key_piece.reshape(block_count, 1024, HEAD_D...  11.3 us
    dot_general x3, matrix products, compute(): jnp.einsum('thk,kd->thd', expo.astype(jnp.bfloat16), value_block, preferr...  11 us
  transfers between devices with their start and end apart: 6, of which 5 were waited for; matrix products, arithmetic and copies ran while one was open for 14% of the time, Pallas kernels for 0%

commit v1 on v0

v1 whole, which is shorter than its diff:
```python
import functools
import math

import jax
import jax.numpy as jnp
from jax import lax
from jax.experimental import pallas as pl
from jax.experimental.pallas import tpu as pltpu
from jax.sharding import PartitionSpec as P

HEAD_DIM = 128
ROWS = 32
GROUP = 8
HALF = 512
SET = 1024
SCALE = math.log2(math.e) / math.sqrt(HEAD_DIM)
LOW = -1e30
NT = (((1,), (1,)), ((), ()))
MESH = pl.DeviceIdType.MESH


def device(x, zz, p, y, c):
    return (x * 2 + zz // 2, ((zz % 2) * 2 + p) * 8 + y * 2 + c)


def kernel(
    q_in, k_in, v_in, owner, slot,
    att, key_cache, value_cache,
    q_land, v_land, kv, acc, top, o_stage, pages,
    kv_send, kv_recv, q_send, q_recv, z_send, z_recv, x_send, x_recv,
    s_send, s_recv, o_send, o_recv, g_send, g_recv,
):
    ctx = lax.axis_index("ctx")
    serve = lax.axis_index("serve")
    x = ctx // 2
    zz = (ctx % 2) * 2 + serve // 16
    p = (serve // 8) % 2
    y = (serve // 2) % 4
    c = serve % 2
    mine = p * 4 + y
    head = y * 2 + p
    x_up, x_down = (x + 1) % 4, (x + 3) % 4
    z_up, z_down = (zz + 1) % 4, (zz + 3) % 4

    def at_x(other):
        return device(other, zz, p, y, c)

    def at_z(other):
        return device(x, other, p, y, c)

    sibling = device(x, zz, p, y, 1 - c)

    def partner(i):
        k = (mine + i) % GROUP
        return k, k // 4, k % 4

    barrier = pltpu.get_barrier_semaphore()
    peers = [sibling, at_x(x_up), at_x(x_down), at_z(z_up), at_z(z_down)]
    for i in range(1, GROUP):
        k, pd, yd = partner(i)
        peers.append(device(x, zz, pd, yd, c))
        peers.append(device(3 - x, zz, pd, yd, c))
    for peer in peers:
        pl.semaphore_signal(barrier, inc=1, device_id=peer, device_id_type=MESH)
    pl.semaphore_wait(barrier, len(peers))

    def cols(start, size):
        return pl.ds(pl.multiple_of(start, 128), size)

    def rows(start):
        return pl.ds(pl.multiple_of(start, ROWS), ROWS)

    def k_copy(i):
        k, pd, yd = partner(i)
        return dict(
            src_ref=k_in.at[:, cols((yd * 2 + pd) * 128, 128)],
            dst_ref=kv.at[0, 0, c, rows(mine * ROWS), :],
        ), device(x, zz, pd, yd, c)

    def v_copy(i):
        k, pd, yd = partner(i)
        return dict(
            src_ref=v_in.at[:, cols((yd * 2 + pd) * 128, 128)],
            dst_ref=v_land.at[mine],
        ), device(x, zz, pd, yd, c)

    def q_copy(i, which):
        k, pd, yd = partner(i)
        return dict(
            src_ref=q_in.at[:, cols((yd * 2 + pd) * 1024 + which * HALF, HALF)],
            dst_ref=q_land.at[which, mine],
        ), device(x if which == 0 else 3 - x, zz, pd, yd, c)

    def remote(refs, to, send, recv):
        return pltpu.make_async_remote_copy(
            **refs, send_sem=send, recv_sem=recv, device_id=to, device_id_type=MESH
        )

    def local(refs, sem):
        return pltpu.make_async_copy(refs["src_ref"], refs["dst_ref"], sem)

    sends = []
    for i in range(1, GROUP):
        for which, make in ((0, k_copy), (1, v_copy)):
            refs, to = make(i)
            sends.append(remote(refs, to, kv_send.at[which, i], kv_recv.at[which]))
    for which, make in ((0, k_copy), (1, v_copy)):
        local(make(0)[0], kv_recv.at[which]).start()
    for copy in sends:
        copy.start()
    for which in range(2):
        for i in range(GROUP):
            refs, to = q_copy(i, which)
            if which == 0 and i == 0:
                local(refs, q_recv.at[0]).start()
            else:
                copy = remote(refs, to, q_send.at[which, i], q_recv.at[which])
                copy.start()
                sends.append(copy)

    acc[...] = jnp.zeros_like(acc)
    top[...] = jnp.full_like(top, LOW)

    def arrived(ref, sem):
        pltpu.make_async_copy(ref, ref, sem).wait()

    def whole(dx, dz):
        return kv.at[dx, dz, c]

    def part(dx, dz, which):
        return kv.at[dx, dz, c, pl.ds(which * 256, 256), :]

    def ring(src, dst, to, send, recv):
        return remote(dict(src_ref=src, dst_ref=dst), to, send, recv)

    def to_sibling(dx, dz):
        n = dx * 4 + dz
        return ring(whole(dx, dz), whole(dx, dz), sibling, s_send.at[n], s_recv.at[n])

    z_copies = [
        ring(whole(0, 0), whole(0, 3), at_z(z_up), z_send.at[0], z_recv.at[0]),
        ring(whole(0, 0), whole(0, 1), at_z(z_down), z_send.at[1], z_recv.at[1]),
        ring(part(0, 3, 0), part(0, 2, 0), at_z(z_up), z_send.at[2], z_recv.at[2]),
        ring(part(0, 1, 1), part(0, 2, 1), at_z(z_down), z_send.at[3], z_recv.at[3]),
    ]

    def x_near(dz, way):
        if way == 0:
            return ring(whole(0, dz), whole(3, dz), at_x(x_up), x_send.at[0, dz], x_recv.at[0, dz])
        return ring(whole(0, dz), whole(1, dz), at_x(x_down), x_send.at[1, dz], x_recv.at[1, dz])

    def x_far(dz, way):
        if way == 0:
            return ring(part(3, dz, 0), part(2, dz, 0), at_x(x_up), x_send.at[2, dz], x_recv.at[2, dz])
        return ring(part(1, dz, 1), part(2, dz, 1), at_x(x_down), x_send.at[3, dz], x_recv.at[3, dz])

    def spread(dz):
        x_near(dz, 0).start()
        x_near(dz, 1).start()
        to_sibling(0, dz).start()

    arrived(kv.at[0, 0, c, pl.ds(0, 256), :], kv_recv.at[0])
    arrived(v_land, kv_recv.at[1])
    v_turned = v_land[...].reshape(256, HEAD_DIM).T
    kv[0, 0, c, 256:384, :] = v_turned[:, 0:128]
    kv[0, 0, c, 384:512, :] = v_turned[:, 128:256]
    z_copies[0].start()
    z_copies[1].start()
    spread(0)
    z_copies[0].wait_recv()
    z_copies[2].start()
    spread(3)
    z_copies[1].wait_recv()
    z_copies[3].start()
    spread(1)
    z_copies[2].wait_recv()
    z_copies[3].wait_recv()
    spread(2)
    arrived(q_land.at[0], q_recv.at[0])
    arrived(q_land.at[1], q_recv.at[1])
    for dz in range(4):
        to_sibling(0, dz).wait_recv()

    def operands(which, dx):
        q = q_land[which]
        q = jnp.concatenate(
            [q[:, :, h * 128 : (h + 1) * 128].reshape(256, HEAD_DIM) for h in range(4)], axis=0
        )
        key = jnp.concatenate(
            [kv[dx, dz, core, 0:256, :] for dz in range(4) for core in range(2)], axis=0
        )
        value = jnp.concatenate(
            [
                kv[dx, dz, core, at : at + 128, :]
                for dz in range(4)
                for core in range(2)
                for at in (256, 384)
            ],
            axis=1,
        )
        value = jnp.concatenate([value, jnp.ones((16, 2048), jnp.bfloat16)], axis=0)
        scores = lax.dot_general(key, q, NT, preferred_element_type=jnp.float32) * SCALE
        return scores, value

    def finish(which, old, new, weights, value):
        product = jnp.dot(value, weights, preferred_element_type=jnp.float32)
        acc[which] = acc[which] * jnp.exp2(old - new)[0:1] + product
        top[which] = new

    def visit_all(which, dx):
        scores, value = operands(which, dx)
        old = top[which]
        new = jnp.maximum(old, jnp.max(scores, axis=0, keepdims=True))
        weights = jnp.exp2(scores - new[0:1]).astype(jnp.bfloat16)
        finish(which, old, new, weights, value)

    def visit_causal(which, dx):
        scores, value = operands(which, dx)
        key_row = lax.broadcasted_iota(jnp.int32, (512, 1), 0)
        key_pos = (key_row % 256 // 32) * 64 + (key_row // 256) * 32 + key_row % 32
        query_row = lax.broadcasted_iota(jnp.int32, (1, SET), 1) % 256
        query_pos = (query_row // 32) * 64 + c * 32 + query_row % 32
        old = top[which]
        pieces = [jnp.where(key_pos <= query_pos, scores[0:512], LOW)]
        new = jnp.maximum(old, jnp.max(pieces[0], axis=0, keepdims=True))
        for dz in range(1, 4):
            pieces.append(scores[dz * 512 : (dz + 1) * 512])
            high = jnp.max(pieces[dz], axis=0, keepdims=True)
            new = jnp.where(zz + dz >= 4, jnp.maximum(new, high), new)
        weights = []
        for dz in range(4):
            base = new[0:1] if dz == 0 else jnp.where(zz + dz >= 4, new[0:1], -LOW)
            weights.append(jnp.exp2(pieces[dz] - base).astype(jnp.bfloat16))
        finish(which, old, new, jnp.concatenate(weights, axis=0), value)

    def place_pages():
        row = lax.broadcasted_iota(jnp.int32, (512, 1), 0)
        k = row // 64
        target = ((zz % 2) * 2 + k // 4) * 32 + (k % 4) * 8 + c * 4 + (row // 16) % 4
        row_key = target * 16 + row % 16
        lane = lax.broadcasted_iota(jnp.int32, (1, 256), 1)
        found_k = jnp.zeros((512, HEAD_DIM), jnp.float32)
        found_v = jnp.zeros((512, HEAD_DIM), jnp.float32)
        for other in range(2):
            low = (zz + other) % 2
            dz = 0 if other == 0 else 1 + 2 * (zz % 2)
            for core in range(2):
                token = jnp.zeros((1, 256), jnp.int32)
                for i in range(16):
                    page = low * 32 + (i // 2) * 4 + core * 2 + i % 2
                    code = owner[page] * 4 + slot[page]
                    token = jnp.where(lane // 16 == i, code, token)
                token = token * 16 + lane % 16
                pick = jnp.where(row_key == token, 1.0, 0.0).astype(jnp.bfloat16)
                found_k += jnp.dot(
                    pick, kv[0, dz, core, 0:256, :],
                    preferred_element_type=jnp.float32,
                )
                turned = jnp.concatenate(
                    [kv[0, dz, core, 256:384, :], kv[0, dz, core, 384:512, :]], axis=1
                )
                found_v += lax.dot_general(pick, turned, NT, preferred_element_type=jnp.float32)
        pages[0] = found_k.astype(jnp.bfloat16).reshape(32, 16, HEAD_DIM)
        pages[1] = found_v.astype(jnp.bfloat16).reshape(32, 16, HEAD_DIM)

    def page_copy(i, which):
        k, pd, yd = partner(i)
        cache = (key_cache, value_cache)[which]
        return dict(
            src_ref=pages.at[which, pl.ds(k * 4, 4)],
            dst_ref=cache.at[:, :, cols(head * 128, 128)],
        ), device(x, zz, pd, yd, c)

    def send_pages():
        for which in range(2):
            local(page_copy(0, which)[0], g_recv.at[which]).start()
            for i in range(1, GROUP):
                refs, to = page_copy(i, which)
                remote(refs, to, g_send.at[which, i], g_recv.at[which]).start()

    def near():
        for dz in (0, 3, 1, 2):
            x_near(dz, 0).wait_recv()
            x_far(dz, 0).start()
            to_sibling(3, dz).start()
            x_near(dz, 1).wait_recv()
            x_far(dz, 1).start()
            to_sibling(1, dz).start()
        for dz in range(4):
            to_sibling(3, dz).wait_recv()
            to_sibling(1, dz).wait_recv()

    def far():
        for dz in (0, 3, 1, 2):
            x_far(dz, 0).wait_recv()
            x_far(dz, 1).wait_recv()
            to_sibling(2, dz).start()
        for dz in range(4):
            to_sibling(2, dz).wait_recv()

    def by_x(t, table):
        value = jnp.int32(0)
        for xi, entries in enumerate(table):
            for ti, entry in enumerate(entries):
                if entry:
                    value = value + jnp.where((x == xi) & (t == ti), entry, 0)
        return value

    sets = ((0, 1, 1, 1, 1), (0, 1, 0, 1, 1), (0, 0, 1, 0, 1), (0, 0, 1, 0, 0))
    steps = ((0, 0, 1, 3, 2), (0, 0, 3, 3, 1), (0, 3, 3, 2, 2), (0, 1, 1, 3, 2))
    causal = ((1, 0, 0, 1, 0), (1, 0, 0, 0, 1), (1, 0, 1, 0, 0), (1, 0, 1, 0, 0))

    def step(t, carry):
        @pl.when(t == 1)
        def _():
            place_pages()
            send_pages()

        @pl.when(t == jnp.where(x >= 2, 1, 2))
        def _():
            near()

        @pl.when(t == 3)
        def _():
            far()

        which = by_x(t, sets)
        dx = by_x(t, steps)
        own = by_x(t, causal)

        @pl.when(own == 1)
        def _():
            visit_causal(which, dx)

        @pl.when(own == 0)
        def _():
            visit_all(which, dx)

        return carry

    lax.fori_loop(0, 5, step, 0)

    def o_copy(i, which):
        k, pd, yd = partner(i)
        return dict(
            src_ref=o_stage.at[which, k],
            dst_ref=att.at[:, cols(head * 1024 + which * HALF, HALF)],
        ), device(x if which == 0 else 3 - x, zz, pd, yd, c)

    for which in range(2):
        total = acc[which, 128:129, :]
        done = acc[which, 0:128, :] / total
        for h in range(4):
            o_stage[which, :, :, h * 128 : (h + 1) * 128] = (
                done[:, h * 256 : (h + 1) * 256].T.astype(jnp.bfloat16).reshape(GROUP, ROWS, HEAD_DIM)
            )
        for i in range(GROUP):
            refs, to = o_copy(i, which)
            if which == 0 and i == 0:
                local(refs, o_recv).start()
            else:
                copy = remote(refs, to, o_send.at[which, i], o_recv)
                copy.start()
                sends.append(copy)

    for copy in sends:
        copy.wait_send()
    for copy in z_copies:
        copy.wait_send()
    for dz in range(4):
        for way in range(2):
            x_near(dz, way).wait_send()
            x_far(dz, way).wait_send()
        for dx in range(4):
            to_sibling(dx, dz).wait_send()
    for which in range(2):
        for i in range(1, GROUP):
            refs, to = page_copy(i, which)
            remote(refs, to, g_send.at[which, i], g_recv.at[which]).wait_send()
    arrived(key_cache, g_recv.at[0])
    arrived(value_cache, g_recv.at[1])
    arrived(att, o_recv)


def shards(queries, key_rows, value_rows, page_owner, page_slot):
    dma = pltpu.SemaphoreType.DMA
    bf16 = jnp.bfloat16
    anywhere = pl.BlockSpec(memory_space=pl.ANY)
    return pl.pallas_call(
        kernel,
        out_shape=(
            jax.ShapeDtypeStruct(queries.shape, bf16),
            jax.ShapeDtypeStruct((4, 16, 1024), bf16),
            jax.ShapeDtypeStruct((4, 16, 1024), bf16),
        ),
        in_specs=[anywhere] * 3 + [pl.BlockSpec(memory_space=pltpu.SMEM)] * 2,
        out_specs=(anywhere,) * 3,
        scratch_shapes=[
            pltpu.VMEM((2, GROUP, ROWS, HALF), bf16),
            pltpu.VMEM((GROUP, ROWS, HEAD_DIM), bf16),
            pltpu.VMEM((4, 4, 2, 512, HEAD_DIM), bf16),
            pltpu.VMEM((2, 144, SET), jnp.float32),
            pltpu.VMEM((2, 8, SET), jnp.float32),
            pltpu.VMEM((2, GROUP, ROWS, HALF), bf16),
            pltpu.VMEM((2, 32, 16, HEAD_DIM), bf16),
            dma((2, GROUP)),
            dma((2,)),
            dma((2, GROUP)),
            dma((2,)),
            dma((4,)),
            dma((4,)),
            dma((4, 4)),
            dma((4, 4)),
            dma((16,)),
            dma((16,)),
            dma((2, GROUP)),
            dma,
            dma((2, GROUP)),
            dma((2,)),
        ],
        compiler_params=pltpu.CompilerParams(
            collective_id=0, has_side_effects=True, vmem_limit_bytes=56 * 2**20
        ),
    )(queries, key_rows, value_rows, page_owner, page_slot)


def solution(mesh):
    whole = P(("ctx", "serve"), None)
    return jax.shard_map(
        shards,
        mesh=mesh,
        in_specs=(whole, whole, whole, P("ctx"), P("ctx")),
        out_specs=(whole, P(("ctx", "serve"), None, None), P(("ctx", "serve"), None, None)),
        check_vma=False,
    )
```

time: 311 us -> 68.8 us (0.22)
  the two profiles are of different devices: /device:TPU:2 before, /device:TPU:1 now
where the time goes in v1:
time: 68.8 us; the launch traced here: 68.6 us
  Pallas kernels  64.5 us (94%)
  local copies, waits for them, and re-layouts  3.51 us (5%)
    pallas_call x1, Pallas kernels, shards(): pl.pallas_call(kernel, out_shape=(jax.ShapeDtypeStruct(queries.shape, bf1...  64.5 us
    unnamed x7, local copies, waits for them, and re-layouts  3.51 us

profile of v1, /device:TPU:1, one launch (start us, length us, event | category | flops | bytes accessed | tf_op | source)
XLA Modules:
  0.0 68.6 jit_solution(7011028986344547810)
XLA Ops:
  0.6 64.5 %shard_map.76 = (bf16[32,8192]{1,0:T(8,128)(2,1)}, bf16[4,16,1024]{2,1,0:T(8,128)(2,1)}, bf16[4,16,1024]{2,1,0:T(8,128)(2,1)}) custom-call(bf16[32,8192]{1,0:T(8,128)(2,1)} %q_in.1, bf16[32,1024]{1,0:T(8,128)(2,1)} %k_in.1, bf16[32,1024]{1,0:T(8,128)(2,1)} %v_in.1, s32[64]{0:T(128)} %owner.1, s32[64]{0:T(128)} %slot.1), custom_call_target="tpu_custom_call" | custom-call | tf_op jit(solution)/shard_map/pallas_call | solution.py:389
  65.1 0.0 copy-start.1
  65.1 1.9 %copy.11 = bf16[32,8192]{1,0:T(8,128)(2,1)} copy(bf16[32,8192]{1,0:T(8,128)(2,1)} %get-tuple-element.6) | data formatting | bytes 1048576
  67.0 0.0 copy-done.1
  67.0 0.0 copy-start
  67.0 0.7 copy.12
  67.7 0.3 copy-done
  68.0 0.7 copy.13
Async XLA Ops:
  65.1 1.9 %copy-start.1 = (bf16[4,16,1024]{2,1,0:T(8,128)(2,1)S(1)}, bf16[4,16,1024]{2,1,0:T(8,128)(2,1)}, u32[]{:S(2)}) copy-start(bf16[4,16,1024]{2,1,0:T(8,128)(2,1)} %get-tuple-element.7) | copy-start | bytes 393220
  67.0 1.0 %copy-start = (bf16[4,16,1024]{2,1,0:T(8,128)(2,1)S(1)}, bf16[4,16,1024]{2,1,0:T(8,128)(2,1)}, u32[]{:S(2)}) copy-start(bf16[4,16,1024]{2,1,0:T(8,128)(2,1)} %get-tuple-element.8) | copy-start | bytes 393220

commit v2 on v0

v2 whole, which is shorter than its diff:
```python
import math

import jax
import jax.numpy as jnp
from jax import lax
from jax.experimental import pallas as pl
from jax.experimental.pallas import tpu as pltpu
from jax.sharding import PartitionSpec as P

HEAD_DIM = 128
ROWS = 32
GROUP = 8
SET = 1024
SCALE = math.log2(math.e) / math.sqrt(HEAD_DIM)
LOW = -1e30
NT = (((1,), (1,)), ((), ()))
MESH = pl.DeviceIdType.MESH


def kernel(
    q_in, k_in, v_in, owner, slot,
    att, key_cache, value_cache,
    q_land, kv_land, kv, acc, top, o_stage, pages, codes,
    kv_send, kv_recv, t_send, t_recv, q_send, q_recv, z_send, z_recv, x_send, x_recv,
    s_send, s_recv, o_send, o_recv, g_send, g_recv,
):
    ctx = lax.axis_index("ctx")
    serve = lax.axis_index("serve")
    x, z_hi = lax.div(ctx, 2), lax.rem(ctx, 2)
    z_lo, low = lax.div(serve, 8), lax.rem(serve, 8)
    y, c = lax.div(low, 2), lax.rem(low, 2)
    z = z_hi * 4 + z_lo
    side, x_odd = lax.div(x, 2), lax.rem(x, 2)
    pair = side + x_odd - 2 * side * x_odd
    x_other = x + 1 - 2 * x_odd
    xs, sides = (x, 3 - x), (side, 1 - side)
    y_odd, y_big = lax.rem(y, 2), lax.div(y, 2)
    ys = (y, y + 1 - 2 * y_odd, y + 2 - 4 * y_big, 3 - y)
    head = y * 2 + side

    def device(xx, zz, yy, cc):
        hi = lax.div(zz, 4)
        return (xx * 2 + hi, (zz - hi * 4) * 8 + yy * 2 + cc)

    def partner(i):
        xx, yy = xs[i // 4], ys[i % 4]
        return (xx * 2 + z_hi, z_lo * 8 + yy * 2 + c), sides[i // 4], yy

    sibling = (ctx, serve + 1 - 2 * c)
    z_ways = (device(x, lax.rem(z + 1, 8), y, c), device(x, lax.rem(z + 7, 8), y, c))
    across = (x_other * 2 + z_hi, serve)

    barrier = pltpu.get_barrier_semaphore()
    peers = [z_ways[0], z_ways[1], across, sibling] + [partner(i)[0] for i in range(1, GROUP)]
    for peer in peers:
        pl.semaphore_signal(barrier, inc=1, device_id=peer, device_id_type=MESH)
    pl.semaphore_wait(barrier, len(peers))

    def cols(start, size):
        return pl.ds(pl.multiple_of(start, 128), size)

    def remote(src, dst, to, send, recv):
        return pltpu.make_async_remote_copy(
            src_ref=src, dst_ref=dst, send_sem=send, recv_sem=recv,
            device_id=to, device_id_type=MESH,
        )

    def local(src, dst, sem):
        return pltpu.make_async_copy(src, dst, sem)

    def arrived(ref, sem):
        pltpu.make_async_copy(ref, ref, sem).wait()

    sends = []
    for i in range(1, GROUP):
        to, their_side, their_y = partner(i)
        for which, ref in ((0, k_in), (1, v_in)):
            src = ref.at[:, cols((their_y * 2 + their_side) * 128, 128)]
            sends.append(
                remote(src, kv_land.at[which, side, y], to, kv_send.at[which, i], kv_recv)
            )
            sends[-1].start()
    for which, ref in ((0, k_in), (1, v_in)):
        local(ref.at[:, cols(head * 128, 128)], kv_land.at[which, side, y], kv_recv).start()
    local(q_in.at[:, cols(head * 1024, 1024)], q_land.at[side, y], q_recv).start()
    for i in range(1, GROUP):
        to, their_side, their_y = partner(i)
        src = q_in.at[:, cols((their_y * 2 + their_side) * 1024, 1024)]
        sends.append(remote(src, q_land.at[side, y], to, q_send.at[i], q_recv))
        sends[-1].start()

    acc[...] = jnp.zeros_like(acc)
    top[...] = jnp.full_like(top, LOW)
    lane = lax.broadcasted_iota(jnp.int32, (8, 128), 1)
    table = jnp.zeros((8, 128), jnp.int32)
    for i in range(64):
        table = jnp.where(lane == i, owner[i] * 4 + slot[i], table)
    codes[0] = table
    sends.append(remote(codes.at[0], codes.at[1], partner(4)[0], t_send, t_recv))
    sends[-1].start()

    def z_copy(i, way, step):
        if way == 0:
            src, dst = lax.rem(8 - step, 8), 7 - step
        else:
            src, dst = step, step + 1
        if isinstance(step, int) and step == 3:
            if i == 0:
                pick = (pl.ds(way, 1),)
            else:
                pick = (2, pl.ds(way * 128, 128))
        else:
            pick = (pl.ds(0, 2),) if i == 0 else (2,)
        return remote(
            kv.at[(src, c) + pick], kv.at[(dst, c) + pick], z_ways[way],
            z_send.at[i, way, step], z_recv.at[i, way, step],
        )

    def first_cross():
        return remote(kv.at[0, c, pair], kv.at[0, c, 2], across, x_send.at[8], x_recv.at[8])

    def cross(dz):
        return remote(kv.at[dz, c, 0], kv.at[dz, c, 3], across, x_send.at[dz], x_recv.at[dz])

    def to_sibling(i, dz):
        ref = kv.at[(dz, c) + ((pl.ds(0, 2),), (2,), (3,))[i]]
        return remote(ref, ref, sibling, s_send.at[i, dz], s_recv.at[i, dz])

    def on_pair(which):
        return pl.when(pair == which)

    arrived(kv_land, kv_recv)
    for which in range(2):
        kv[0, c, which, 0:128, :] = kv_land[0, which].reshape(128, HEAD_DIM)
        kv[0, c, which, 128:256, :] = kv_land[1, which].reshape(128, HEAD_DIM).T
    first_cross().start()
    z_copy(0, 0, 0).start()
    z_copy(0, 1, 0).start()
    to_sibling(0, 0).start()

    @on_pair(1)
    def _():
        cross(0).start()

    first_cross().wait_recv()
    z_copy(1, 0, 0).start()
    z_copy(1, 1, 0).start()
    to_sibling(1, 0).start()

    @on_pair(0)
    def _():
        cross(0).wait_recv()
        to_sibling(2, 0).start()

    def attend(which, blocks):
        q = q_land[which]
        q = jnp.concatenate(
            [q[:, :, h * 128 : (h + 1) * 128].reshape(128, HEAD_DIM) for h in range(8)], axis=0
        )
        scores = []
        for role, dzs, kind in blocks:
            key = jnp.concatenate(
                [kv[dz, core, role, 0:128, :] for dz in dzs for core in range(2)], axis=0
            )
            part = lax.dot_general(key, q, NT, preferred_element_type=jnp.float32)
            if kind == "diagonal":
                row = lax.broadcasted_iota(jnp.int32, (256, 1), 0)
                key_pos = (row % 128 // 32) * 64 + (row // 128) * 32 + row % 32
                token = lax.broadcasted_iota(jnp.int32, (1, SET), 1) % 128
                query_pos = (token // 32) * 64 + c * 32 + token % 32
                part = jnp.where(key_pos <= query_pos, part, LOW)
            scores.append(part)
        old, total = top[which], acc[which]
        for (role, dzs, kind), part in zip(blocks, scores):
            if kind == "earlier":
                new, weights = old, []
                for n, dz in enumerate(dzs):
                    high = jnp.max(part[n * 256 : (n + 1) * 256], axis=0, keepdims=True)
                    new = jnp.where(z + dz >= 8, jnp.maximum(new, high), new)
                for n, dz in enumerate(dzs):
                    base = jnp.where(z + dz >= 8, new[0:1], -LOW)
                    weights.append(
                        jnp.exp2((part[n * 256 : (n + 1) * 256] - base) * SCALE).astype(jnp.bfloat16)
                    )
                weights = jnp.concatenate(weights, axis=0)
            else:
                new = jnp.maximum(old, jnp.max(part, axis=0, keepdims=True))
                weights = jnp.exp2((part - new[0:1]) * SCALE).astype(jnp.bfloat16)
            value = jnp.concatenate(
                [kv[dz, core, role, 128:256, :] for dz in dzs for core in range(2)], axis=1
            )
            value = jnp.concatenate([value, jnp.ones((16, value.shape[1]), jnp.bfloat16)], axis=0)
            product = jnp.dot(value, weights, preferred_element_type=jnp.float32)
            total = total * jnp.exp2((old - new) * SCALE)[0:1] + product
            old = new
        top[which] = old
        acc[which] = total

    def first_unit(dzs, kind):
        attend(pair, [(pair, dzs, kind)])

    def second_unit(dzs):
        attend(1, [(0, dzs, "all"), (2, dzs, "all")])

    def third_unit(dzs, kind):
        attend(1 - pair, [(3 - pair, dzs, "all"), (1 - pair, dzs, kind)])

    def place_pages():
        for which in range(2):
            code = jnp.where(side == which, codes[0], codes[1])
            spot = lax.broadcasted_iota(jnp.int32, (128, 1024), 1)
            entry = lax.broadcasted_iota(jnp.int32, (128, 1024), 0)
            page = (spot // 256) * 16 + (spot % 128 // 32) * 4 + (spot % 256 // 128) * 2 + spot % 32 // 16
            spread = jnp.where(entry == page, 1.0, 0.0).astype(jnp.bfloat16)
            token = jnp.dot(code.astype(jnp.bfloat16), spread, preferred_element_type=jnp.float32)
            token = token[0:1].astype(jnp.int32) * 16 + spot[0:1] % 16
            row = lax.broadcasted_iota(jnp.int32, (256, 1), 0)
            target = (z_lo * 8 + (row // 64) * 2 + c) * 4 + row // 16 % 4
            pick = jnp.where(target * 16 + row % 16 == token, 1.0, 0.0).astype(jnp.bfloat16)
            parts = [(lax.rem(lo + 8 - z_lo, 8), core) for lo in range(4) for core in range(2)]
            key = jnp.concatenate([kv[dz, core, which, 0:128, :] for dz, core in parts], axis=0)
            value = jnp.concatenate([kv[dz, core, which, 128:256, :] for dz, core in parts], axis=1)
            found = jnp.dot(pick, key, preferred_element_type=jnp.float32)
            pages[0, which] = found.astype(jnp.bfloat16).reshape(16, 16, HEAD_DIM)
            found = lax.dot_general(pick, value, NT, preferred_element_type=jnp.float32)
            pages[1, which] = found.astype(jnp.bfloat16).reshape(16, 16, HEAD_DIM)

    def page_copy(i, which):
        to, their_side, their_y = partner(i)
        cache = (key_cache, value_cache)[which]
        src = pages.at[which, their_side, pl.ds(their_y * 4, 4)]
        dst = cache.at[:, :, cols(head * 128, 128)]
        if i == 0:
            return local(src, dst, g_recv.at[which])
        return remote(src, dst, to, g_send.at[which, i], g_recv.at[which])

    def o_copy(which, j):
        src, dst = o_stage.at[which, ys[j]], att.at[:, cols(head * 1024, 1024)]
        xx = jnp.where(side == which, x, 3 - x)
        return src, dst, (xx * 2 + z_hi, z_lo * 8 + ys[j] * 2 + c), o_send.at[which, ys[j]]

    def finish(which):
        done = acc[which, 0:128, :] / acc[which, 128:129, :]
        for h in range(8):
            o_stage[which, :, :, h * 128 : (h + 1) * 128] = (
                done[:, h * 128 : (h + 1) * 128].T.astype(jnp.bfloat16).reshape(4, ROWS, HEAD_DIM)
            )
        for j in range(1, 4):
            src, dst, to, sem = o_copy(which, j)
            remote(src, dst, to, sem, o_recv).start()
        src, dst, to, sem = o_copy(which, 0)

        @pl.when(side == which)
        def _():
            local(src, dst, o_recv).start()

        @pl.when(side != which)
        def _():
            remote(src, dst, to, sem, o_recv).start()

    arrived(q_land, q_recv)
    to_sibling(0, 0).wait_recv()
    first_unit((0,), "diagonal")
    to_sibling(1, 0).wait_recv()
    second_unit((0,))

    @on_pair(0)
    def _():
        to_sibling(2, 0).wait_recv()

    third_unit((0,), "diagonal")

    def stage(d, carry):
        both = (8 - d, d)
        for i in range(2):
            for way in range(2):
                z_copy(i, way, d - 1).wait_recv()

                @pl.when(d < 3)
                def _():
                    z_copy(i, way, d).start()

                @pl.when(d == 3)
                def _():
                    z_copy(i, way, 3).start()

                to_sibling(i, both[way]).start()
                if i == 0:

                    @on_pair(1)
                    def _():
                        cross(both[way]).start()

        to_sibling(0, 8 - d).wait_recv()
        to_sibling(0, d).wait_recv()
        first_unit(both, "earlier")
        to_sibling(1, 8 - d).wait_recv()
        to_sibling(1, d).wait_recv()
        second_unit(both)

        @on_pair(0)
        def _():
            for dz in both:
                cross(dz).wait_recv()
                to_sibling(2, dz).start()
            for dz in both:
                to_sibling(2, dz).wait_recv()

        third_unit(both, "earlier")
        return carry

    lax.fori_loop(1, 4, stage, 0)

    z_copy(0, 0, 3).wait_recv()
    z_copy(0, 1, 3).wait_recv()
    to_sibling(0, 4).start()

    @on_pair(1)
    def _():
        cross(4).start()

    z_copy(1, 0, 3).wait_recv()
    z_copy(1, 1, 3).wait_recv()
    to_sibling(1, 4).start()
    arrived(codes.at[1], t_recv)
    place_pages()
    for which in range(2):
        for i in range(GROUP):
            page_copy(i, which).start()
    to_sibling(0, 4).wait_recv()
    first_unit((4,), "earlier")

    @on_pair(0)
    def _():
        finish(0)

    to_sibling(1, 4).wait_recv()
    second_unit((4,))

    @on_pair(1)
    def _():
        finish(1)

    @on_pair(0)
    def _():
        cross(4).wait_recv()
        to_sibling(2, 4).start()
        to_sibling(2, 4).wait_recv()

    third_unit((4,), "earlier")
    finish(1 - pair)

    for copy in sends:
        copy.wait_send()
    first_cross().wait_send()
    for way in range(2):
        for step in range(4):
            z_copy(0, way, step).wait_send()
            z_copy(1, way, step).wait_send()
    for dz in range(8):
        to_sibling(0, dz).wait_send()
        to_sibling(1, dz).wait_send()

    @on_pair(0)
    def _():
        for dz in range(8):
            to_sibling(2, dz).wait_send()

    @on_pair(1)
    def _():
        for dz in range(8):
            cross(dz).wait_send()

    for which in range(2):
        for i in range(1, GROUP):
            page_copy(i, which).wait_send()
    for which in range(2):
        for j in range(4):
            src, dst, to, sem = o_copy(which, j)
            if j == 0:

                @pl.when(side != which)
                def _():
                    remote(src, dst, to, sem, o_recv).wait_send()

            else:
                remote(src, dst, to, sem, o_recv).wait_send()
    arrived(key_cache, g_recv.at[0])
    arrived(value_cache, g_recv.at[1])
    arrived(att, o_recv)


def shards(queries, key_rows, value_rows, page_owner, page_slot):
    dma = pltpu.SemaphoreType.DMA
    bf16 = jnp.bfloat16
    anywhere = pl.BlockSpec(memory_space=pl.ANY)
    return pl.pallas_call(
        kernel,
        out_shape=(
            jax.ShapeDtypeStruct(queries.shape, bf16),
            jax.ShapeDtypeStruct((4, 16, 1024), bf16),
            jax.ShapeDtypeStruct((4, 16, 1024), bf16),
        ),
        in_specs=[anywhere] * 3 + [pl.BlockSpec(memory_space=pltpu.SMEM)] * 2,
        out_specs=(anywhere,) * 3,
        scratch_shapes=[
            pltpu.VMEM((2, 4, ROWS, SET), bf16),
            pltpu.VMEM((2, 2, 4, ROWS, HEAD_DIM), bf16),
            pltpu.VMEM((8, 2, 4, 256, HEAD_DIM), bf16),
            pltpu.VMEM((2, 144, SET), jnp.float32),
            pltpu.VMEM((2, 8, SET), jnp.float32),
            pltpu.VMEM((2, 4, ROWS, SET), bf16),
            pltpu.VMEM((2, 2, 16, 16, HEAD_DIM), bf16),
            pltpu.VMEM((2, 8, 128), jnp.int32),
            dma((2, GROUP)),
            dma,
            dma,
            dma,
            dma((GROUP,)),
            dma,
            dma((2, 2, 4)),
            dma((2, 2, 4)),
            dma((9,)),
            dma((9,)),
            dma((3, 8)),
            dma((3, 8)),
            dma((2, 4)),
            dma,
            dma((2, GROUP)),
            dma((2,)),
        ],
        compiler_params=pltpu.CompilerParams(
            collective_id=0, has_side_effects=True, vmem_limit_bytes=56 * 2**20
        ),
    )(queries, key_rows, value_rows, page_owner, page_slot)


def solution(mesh):
    whole = P(("ctx", "serve"), None)
    return jax.shard_map(
        shards,
        mesh=mesh,
        in_specs=(whole, whole, whole, P("ctx"), P("ctx")),
        out_specs=(whole, P(("ctx", "serve"), None, None), P(("ctx", "serve"), None, None)),
        check_vma=False,
    )
```

time: 311 us -> 61 us (0.20)
  the two profiles are of different devices: /device:TPU:2 before, /device:TPU:6 now
where the time goes in v2:
time: 61 us; the launch traced here: 60.8 us
  Pallas kernels  56.7 us (93%)
  local copies, waits for them, and re-layouts  3.51 us (6%)
  between operations  0.65 us (1%)
    pallas_call x1, Pallas kernels, shards(): pl.pallas_call(kernel, out_shape=(jax.ShapeDtypeStruct(queries.shape, bf1...  56.7 us
    unnamed x7, local copies, waits for them, and re-layouts  3.51 us

profile of v2, /device:TPU:6, one launch (start us, length us, event | category | flops | bytes accessed | tf_op | source)
XLA Modules:
  0.0 60.8 jit_solution(12057642089757027785)
XLA Ops:
  0.6 56.7 %shard_map.76 = (bf16[32,8192]{1,0:T(8,128)(2,1)}, bf16[4,16,1024]{2,1,0:T(8,128)(2,1)}, bf16[4,16,1024]{2,1,0:T(8,128)(2,1)}) custom-call(bf16[32,8192]{1,0:T(8,128)(2,1)} %q_in.1, bf16[32,1024]{1,0:T(8,128)(2,1)} %k_in.1, bf16[32,1024]{1,0:T(8,128)(2,1)} %v_in.1, s32[64]{0:T(128)} %owner.1, s32[64]{0:T(128)} %slot.1), custom_call_target="tpu_custom_call" | custom-call | tf_op jit(solution)/shard_map/pallas_call | solution.py:397
  57.3 0.0 copy-start.1
  57.3 1.9 %copy.11 = bf16[32,8192]{1,0:T(8,128)(2,1)} copy(bf16[32,8192]{1,0:T(8,128)(2,1)} %get-tuple-element.6) | data formatting | bytes 1048576
  59.2 0.0 copy-done.1
  59.2 0.0 copy-start
  59.2 0.7 %copy.12 = bf16[4,16,1024]{2,1,0:T(8,128)(2,1)} copy(bf16[4,16,1024]{2,1,0:T(8,128)(2,1)S(1)} %copy-done.1) | data formatting | bytes 262144
  59.9 0.3 copy-done
  60.2 0.7 %copy.13 = bf16[4,16,1024]{2,1,0:T(8,128)(2,1)} copy(bf16[4,16,1024]{2,1,0:T(8,128)(2,1)S(1)} %copy-done) | data formatting | bytes 262144
Async XLA Ops:
  57.3 1.9 %copy-start.1 = (bf16[4,16,1024]{2,1,0:T(8,128)(2,1)S(1)}, bf16[4,16,1024]{2,1,0:T(8,128)(2,1)}, u32[]{:S(2)}) copy-start(bf16[4,16,1024]{2,1,0:T(8,128)(2,1)} %get-tuple-element.7) | copy-start | bytes 393220
  59.2 1.0 %copy-start = (bf16[4,16,1024]{2,1,0:T(8,128)(2,1)S(1)}, bf16[4,16,1024]{2,1,0:T(8,128)(2,1)}, u32[]{:S(2)}) copy-start(bf16[4,16,1024]{2,1,0:T(8,128)(2,1)} %get-tuple-element.8) | copy-start | bytes 393220

commit v3 on v2

v3 whole, which is shorter than its diff:
```python
import math

import jax
import jax.numpy as jnp
from jax import lax
from jax.experimental import pallas as pl
from jax.experimental.pallas import tpu as pltpu
from jax.sharding import PartitionSpec as P

HEAD_DIM = 128
ROWS = 32
GROUP = 8
SET = 1024
HALF = 512
SCALE = math.log2(math.e) / math.sqrt(HEAD_DIM)
LOW = -1e30
NT = (((1,), (1,)), ((), ()))
MESH = pl.DeviceIdType.MESH


def kernel(
    q_in, k_in, v_in, owner, slot,
    att, key_cache, value_cache,
    q_here, kv_here, q_land, kv_land, kv, acc, top, o_stage, pages, codes,
    in_sem, kv_send, kv_recv, t_send, t_recv, q_send, q_recv, z_send, z_recv, x_send, x_recv,
    s_send, s_recv, o_send, o_recv, g_send, g_recv,
):
    ctx = lax.axis_index("ctx")
    serve = lax.axis_index("serve")
    x, z_hi = lax.div(ctx, 2), lax.rem(ctx, 2)
    z_lo, low = lax.div(serve, 8), lax.rem(serve, 8)
    y, c = lax.div(low, 2), lax.rem(low, 2)
    z = z_hi * 4 + z_lo
    side, x_odd = lax.div(x, 2), lax.rem(x, 2)
    pair = side + x_odd - 2 * side * x_odd
    x_other = x + 1 - 2 * x_odd
    xs, sides = (x, 3 - x), (side, 1 - side)
    y_odd, y_big = lax.rem(y, 2), lax.div(y, 2)
    ys = (y, y + 1 - 2 * y_odd, y + 2 - 4 * y_big, 3 - y)
    head = y * 2 + side

    def device(xx, zz, yy, cc):
        hi = lax.div(zz, 4)
        return (xx * 2 + hi, (zz - hi * 4) * 8 + yy * 2 + cc)

    def partner(i):
        xx, yy = xs[i // 4], ys[i % 4]
        return (xx * 2 + z_hi, z_lo * 8 + yy * 2 + c), sides[i // 4], yy

    sibling = (ctx, serve + 1 - 2 * c)
    z_ways = (device(x, lax.rem(z + 1, 8), y, c), device(x, lax.rem(z + 7, 8), y, c))
    across = (x_other * 2 + z_hi, serve)

    loads = [
        pltpu.make_async_copy(k_in, kv_here.at[0], in_sem.at[0]),
        pltpu.make_async_copy(v_in, kv_here.at[1], in_sem.at[1]),
        pltpu.make_async_copy(q_in, q_here, in_sem.at[2]),
    ]
    barrier = pltpu.get_barrier_semaphore()
    peers = [z_ways[0], z_ways[1], across, sibling] + [partner(i)[0] for i in range(1, GROUP)]
    for peer in peers:
        pl.semaphore_signal(barrier, inc=1, device_id=peer, device_id_type=MESH)
    for load in loads:
        load.start()
    acc[...] = jnp.zeros_like(acc)
    top[...] = jnp.full_like(top, LOW)
    lane = lax.broadcasted_iota(jnp.int32, (8, 128), 1)
    table = jnp.zeros((8, 128), jnp.int32)
    for i in range(64):
        table = jnp.where(lane == i, owner[i] * 4 + slot[i], table)
    codes[0] = table
    for load in loads:
        load.wait()
    pl.semaphore_wait(barrier, len(peers))

    def cols(start, size):
        return pl.ds(pl.multiple_of(start, 128), size)

    def remote(src, dst, to, send, recv):
        return pltpu.make_async_remote_copy(
            src_ref=src, dst_ref=dst, send_sem=send, recv_sem=recv,
            device_id=to, device_id_type=MESH,
        )

    def local(src, dst, sem):
        return pltpu.make_async_copy(src, dst, sem)

    def arrived(ref, sem):
        pltpu.make_async_copy(ref, ref, sem).wait()

    sends = []
    for i in (6, 5, 7, 2, 4, 1, 3):
        to, their_side, their_y = partner(i)
        for which in range(2):
            src = kv_here.at[which, :, cols((their_y * 2 + their_side) * 128, 128)]
            sends.append(
                remote(src, kv_land.at[which, side, y], to, kv_send.at[which, i], kv_recv)
            )
            sends[-1].start()
    for which in range(2):
        src = kv_here.at[which, :, cols(head * 128, 128)]
        local(src, kv_land.at[which, side, y], kv_recv).start()
    for half in range(2):
        src = q_here.at[:, cols(head * 1024 + half * HALF, HALF)]
        local(src, q_land.at[half, side, y], q_recv.at[half]).start()
        for i in (6, 5, 7, 2, 4, 1, 3):
            to, their_side, their_y = partner(i)
            src = q_here.at[:, cols((their_y * 2 + their_side) * 1024 + half * HALF, HALF)]
            sends.append(
                remote(src, q_land.at[half, side, y], to, q_send.at[half, i], q_recv.at[half])
            )
            sends[-1].start()
    sends.append(remote(codes.at[0], codes.at[1], partner(4)[0], t_send, t_recv))
    sends[-1].start()

    def z_copy(role, way, step):
        if way == 0:
            src, dst = lax.rem(8 - step, 8), 7 - step
        else:
            src, dst = step, step + 1
        pick = (role, pl.ds(way * 128, 128)) if isinstance(step, int) and step == 3 else (role,)
        return remote(
            kv.at[(src, c) + pick], kv.at[(dst, c) + pick], z_ways[way],
            z_send.at[role, way, step], z_recv.at[role, way, step],
        )

    def first_cross():
        return remote(kv.at[0, c, 1], kv.at[0, c, 2], across, x_send.at[8], x_recv.at[8])

    def cross(dz):
        return remote(
            kv.at[dz, c, 0], kv.at[dz, c, 2 + pair], across, x_send.at[dz], x_recv.at[dz]
        )

    def to_sibling(role, dz):
        ref = kv.at[dz, c, role]
        return remote(ref, ref, sibling, s_send.at[role, dz], s_recv.at[role, dz])

    def on_pair(which):
        return pl.when(pair == which)

    def take(role, d):
        for way, dz in ((0, 8 - d), (1, d)):
            z_copy(role, way, d - 1).wait_recv()

            @pl.when(d < 3)
            def _():
                z_copy(role, way, d).start()

            @pl.when(d == 3)
            def _():
                z_copy(role, way, 3).start()

            if role == 0:
                cross(dz).start()
            to_sibling(role, dz).start()

    def take_last(role):
        z_copy(role, 0, 3).wait_recv()
        z_copy(role, 1, 3).wait_recv()
        if role == 0:
            cross(4).start()
        to_sibling(role, 4).start()

    def crossed(dzs):
        for dz in dzs:
            cross(dz).wait_recv()
            to_sibling(3 - pair, dz).start()

    def heard(roles, dzs):
        for role in roles:
            for dz in dzs:
                to_sibling(role, dz).wait_recv()

    arrived(kv_land, kv_recv)
    for which in range(2):
        kv[0, c, which, 0:128, :] = kv_land[0, which].reshape(128, HEAD_DIM)
        kv[0, c, which, 128:256, :] = kv_land[1, which].reshape(128, HEAD_DIM).T

    @on_pair(1)
    def _():
        first_cross().start()

    for role in range(2):
        z_copy(role, 0, 0).start()
        z_copy(role, 1, 0).start()
        to_sibling(role, 0).start()
        if role == 0:
            cross(0).start()

    @on_pair(0)
    def _():
        first_cross().wait_recv()
        z_copy(2, 0, 0).start()
        z_copy(2, 1, 0).start()
        to_sibling(2, 0).start()

    crossed((0,))

    def queries_of(which, heads):
        parts = []
        for h in heads:
            q = q_land[h // 4, which, :, :, h % 4 * 128 : (h % 4 + 1) * 128]
            parts.append(q.reshape(128, HEAD_DIM))
        return jnp.concatenate(parts, axis=0)

    def attend(which, heads, blocks):
        q = queries_of(which, heads)
        spot = slice(heads[0] * 128, heads[-1] * 128 + 128)
        scores = []
        for role, dzs, kind in blocks:
            key = jnp.concatenate(
                [kv[dz, core, role, 0:128, :] for dz in dzs for core in range(2)], axis=0
            )
            part = lax.dot_general(key, q, NT, preferred_element_type=jnp.float32)
            if kind == "diagonal":
                row = lax.broadcasted_iota(jnp.int32, (256, 1), 0)
                key_pos = (row % 128 // 32) * 64 + (row // 128) * 32 + row % 32
                token = lax.broadcasted_iota(jnp.int32, (1, q.shape[0]), 1) % 128
                query_pos = (token // 32) * 64 + c * 32 + token % 32
                part = jnp.where(key_pos <= query_pos, part, LOW)
            scores.append(part)
        old, total = top[which, :, spot], acc[which, :, spot]
        for (role, dzs, kind), part in zip(blocks, scores):
            if kind == "earlier":
                new, weights = old, []
                for n, dz in enumerate(dzs):
                    high = jnp.max(part[n * 256 : (n + 1) * 256], axis=0, keepdims=True)
                    new = jnp.where(z + dz >= 8, jnp.maximum(new, high), new)
                for n, dz in enumerate(dzs):
                    base = jnp.where(z + dz >= 8, new[0:1], -LOW)
                    weights.append(
                        jnp.exp2((part[n * 256 : (n + 1) * 256] - base) * SCALE).astype(jnp.bfloat16)
                    )
                weights = jnp.concatenate(weights, axis=0)
            else:
                new = jnp.maximum(old, jnp.max(part, axis=0, keepdims=True))
                weights = jnp.exp2((part - new[0:1]) * SCALE).astype(jnp.bfloat16)
            value = jnp.concatenate(
                [kv[dz, core, role, 128:256, :] for dz in dzs for core in range(2)], axis=1
            )
            value = jnp.concatenate([value, jnp.ones((16, value.shape[1]), jnp.bfloat16)], axis=0)
            product = jnp.dot(value, weights, preferred_element_type=jnp.float32)
            total = total * jnp.exp2((old - new) * SCALE)[0:1] + product
            old = new
        top[which, :, spot] = old
        acc[which, :, spot] = total

    def own_units(heads, dzs, kind):
        attend(1, heads, [(0, dzs, "all"), (1, dzs, kind)])
        attend(0, heads, [(0, dzs, kind)])

    def other_units(heads, dzs):
        @on_pair(0)
        def _():
            attend(1, heads, [(2, dzs, "all"), (3, dzs, "all")])

        @on_pair(1)
        def _():
            attend(1, heads, [(2, dzs, "all")])
            attend(0, heads, [(2, dzs, "all")])

    everything = range(8)
    halves = (range(4), range(4, 8))

    def place_pages():
        for which in range(2):
            code = jnp.where(side == which, codes[0], codes[1])
            spot = lax.broadcasted_iota(jnp.int32, (128, 1024), 1)
            entry = lax.broadcasted_iota(jnp.int32, (128, 1024), 0)
            page = (spot // 256) * 16 + (spot % 128 // 32) * 4 + (spot % 256 // 128) * 2 + spot % 32 // 16
            spread = jnp.where(entry == page, 1.0, 0.0).astype(jnp.bfloat16)
            token = jnp.dot(code.astype(jnp.bfloat16), spread, preferred_element_type=jnp.float32)
            token = token[0:1].astype(jnp.int32) * 16 + spot[0:1] % 16
            row = lax.broadcasted_iota(jnp.int32, (256, 1), 0)
            target = (z_lo * 8 + (row // 64) * 2 + c) * 4 + row // 16 % 4
            pick = jnp.where(target * 16 + row % 16 == token, 1.0, 0.0).astype(jnp.bfloat16)
            parts = [(lax.rem(lo + 8 - z_lo, 8), core) for lo in range(4) for core in range(2)]
            key = jnp.concatenate([kv[dz, core, which, 0:128, :] for dz, core in parts], axis=0)
            value = jnp.concatenate([kv[dz, core, which, 128:256, :] for dz, core in parts], axis=1)
            found = jnp.dot(pick, key, preferred_element_type=jnp.float32)
            pages[0, which] = found.astype(jnp.bfloat16).reshape(16, 16, HEAD_DIM)
            found = lax.dot_general(pick, value, NT, preferred_element_type=jnp.float32)
            pages[1, which] = found.astype(jnp.bfloat16).reshape(16, 16, HEAD_DIM)

    def page_copy(i, which):
        to, their_side, their_y = partner(i)
        cache = (key_cache, value_cache)[which]
        src = pages.at[which, their_side, pl.ds(their_y * 4, 4)]
        dst = cache.at[:, :, cols(head * 128, 128)]
        if i == 0:
            return local(src, dst, g_recv.at[which])
        return remote(src, dst, to, g_send.at[which, i], g_recv.at[which])

    def o_copy(which, half, j):
        src = o_stage.at[which, half, ys[j]]
        dst = att.at[:, cols(head * 1024 + half * HALF, HALF)]
        xx = jnp.where(side == which, x, 3 - x)
        to = (xx * 2 + z_hi, z_lo * 8 + ys[j] * 2 + c)
        return src, dst, to, o_send.at[which, half, ys[j]]

    def finish(which, half):
        done = acc[which, 0:128, half * 512 : (half + 1) * 512]
        done = done / acc[which, 128:129, half * 512 : (half + 1) * 512]
        for h in range(4):
            o_stage[which, half, :, :, h * 128 : (h + 1) * 128] = (
                done[:, h * 128 : (h + 1) * 128].T.astype(jnp.bfloat16).reshape(4, ROWS, HEAD_DIM)
            )

    def send_finished(which, half):
        for j in (2, 1, 3):
            src, dst, to, sem = o_copy(which, half, j)
            remote(src, dst, to, sem, o_recv).start()
        src, dst, to, sem = o_copy(which, half, 0)

        @pl.when(side == which)
        def _():
            local(src, dst, o_recv).start()

        @pl.when(side != which)
        def _():
            remote(src, dst, to, sem, o_recv).start()

    heard((0, 1), (0,))
    arrived(q_land.at[0], q_recv.at[0])
    own_units(halves[0], (0,), "diagonal")
    take(0, 1)
    take(1, 1)
    heard((2,), (0,))

    @on_pair(0)
    def _():
        heard((3,), (0,))

    other_units(halves[0], (0,))
    arrived(q_land.at[1], q_recv.at[1])
    own_units(halves[1], (0,), "diagonal")
    other_units(halves[1], (0,))

    def stage(d, carry):
        both = (8 - d, d)

        @on_pair(0)
        def _():
            take(2, d)

        heard((0, 1), both)
        own_units(everything, both, "earlier")
        crossed(both)

        @pl.when(d < 3)
        def _():
            take(0, d + 1)
            take(1, d + 1)

        @pl.when(d == 3)
        def _():
            take_last(0)
            take_last(1)
            arrived(codes.at[1], t_recv)
            place_pages()
            for which in range(2):
                for i in range(GROUP):
                    page_copy(i, which).start()

        heard((2,), both)

        @on_pair(0)
        def _():
            heard((3,), both)

        other_units(everything, both)
        return carry

    lax.fori_loop(1, 4, stage, 0)

    @on_pair(0)
    def _():
        take_last(2)

    heard((0, 1), (4,))
    own_units(halves[0], (4,), "earlier")
    crossed((4,))
    own_units(halves[1], (4,), "earlier")
    heard((2,), (4,))

    @on_pair(0)
    def _():
        heard((3,), (4,))

    for half in range(2):
        other_units(halves[half], (4,))
        for which in range(2):
            finish(which, half)
        for which in range(2):
            send_finished(which, half)

    for copy in sends:
        copy.wait_send()
    for role in range(2):
        for way in range(2):
            for step in range(4):
                z_copy(role, way, step).wait_send()
    for dz in range(8):
        cross(dz).wait_send()
        for role in range(3):
            to_sibling(role, dz).wait_send()

    @on_pair(0)
    def _():
        for way in range(2):
            for step in range(4):
                z_copy(2, way, step).wait_send()
        for dz in range(8):
            to_sibling(3, dz).wait_send()

    @on_pair(1)
    def _():
        first_cross().wait_send()

    for which in range(2):
        for i in range(1, GROUP):
            page_copy(i, which).wait_send()
    for which in range(2):
        for half in range(2):
            for j in range(1, 4):
                src, dst, to, sem = o_copy(which, half, j)
                remote(src, dst, to, sem, o_recv).wait_send()

        @pl.when(side != which)
        def _():
            for half in range(2):
                src, dst, to, sem = o_copy(which, half, 0)
                remote(src, dst, to, sem, o_recv).wait_send()

    arrived(key_cache, g_recv.at[0])
    arrived(value_cache, g_recv.at[1])
    arrived(att, o_recv)


def move(att, key_cache, value_cache, att_out, key_out, value_out):
    att_out[...] = att[...]
    key_out[...] = key_cache[...]
    value_out[...] = value_cache[...]


def shards(queries, key_rows, value_rows, page_owner, page_slot):
    dma = pltpu.SemaphoreType.DMA
    bf16 = jnp.bfloat16
    anywhere = pl.BlockSpec(memory_space=pl.ANY)
    held = pl.pallas_call(
        kernel,
        out_shape=(
            jax.ShapeDtypeStruct(queries.shape, bf16),
            jax.ShapeDtypeStruct((4, 16, 1024), bf16),
            jax.ShapeDtypeStruct((4, 16, 1024), bf16),
        ),
        in_specs=[anywhere] * 3 + [pl.BlockSpec(memory_space=pltpu.SMEM)] * 2,
        out_specs=(anywhere,) * 3,
        scratch_shapes=[
            pltpu.VMEM((ROWS, 8192), bf16),
            pltpu.VMEM((2, ROWS, 1024), bf16),
            pltpu.VMEM((2, 2, 4, ROWS, HALF), bf16),
            pltpu.VMEM((2, 2, 4, ROWS, HEAD_DIM), bf16),
            pltpu.VMEM((8, 2, 4, 256, HEAD_DIM), bf16),
            pltpu.VMEM((2, 144, SET), jnp.float32),
            pltpu.VMEM((2, 8, SET), jnp.float32),
            pltpu.VMEM((2, 2, 4, ROWS, HALF), bf16),
            pltpu.VMEM((2, 2, 16, 16, HEAD_DIM), bf16),
            pltpu.VMEM((2, 8, 128), jnp.int32),
            dma((3,)),
            dma((2, GROUP)),
            dma,
            dma,
            dma,
            dma((2, GROUP)),
            dma((2,)),
            dma((3, 2, 4)),
            dma((3, 2, 4)),
            dma((9,)),
            dma((9,)),
            dma((4, 8)),
            dma((4, 8)),
            dma((2, 2, 4)),
            dma,
            dma((2, GROUP)),
            dma((2,)),
        ],
        compiler_params=pltpu.CompilerParams(
            collective_id=0, has_side_effects=True, vmem_limit_bytes=56 * 2**20
        ),
    )(queries, key_rows, value_rows, page_owner, page_slot)
    return pl.pallas_call(
        move,
        out_shape=tuple(jax.ShapeDtypeStruct(a.shape, bf16) for a in held),
        in_specs=[pl.BlockSpec(memory_space=pltpu.VMEM)] * 3,
        out_specs=(pl.BlockSpec(memory_space=pltpu.VMEM),) * 3,
    )(*held)


def solution(mesh):
    whole = P(("ctx", "serve"), None)
    return jax.shard_map(
        shards,
        mesh=mesh,
        in_specs=(whole, whole, whole, P("ctx"), P("ctx")),
        out_specs=(whole, P(("ctx", "serve"), None, None), P(("ctx", "serve"), None, None)),
        check_vma=False,
    )
```

time: 61 us -> 54.5 us (0.89)
  the two profiles are of different devices: /device:TPU:6 before, /device:TPU:1 now
where the time goes in v3:
time: 54.5 us; the launch traced here: 54.3 us
  Pallas kernels  53.7 us (99%)
  between operations  0.64 us (1%)
    pallas_call x1, Pallas kernels, shards(): pl.pallas_call(kernel, out_shape=(jax.ShapeDtypeStruct(queries.shape, bf1...  51.7 us
    pallas_call x1, Pallas kernels, shards(): pl.pallas_call(move, out_shape=tuple((jax.ShapeDtypeStruct(a.shape, bf16)...  2.01 us

profile of v3, /device:TPU:1, one launch (start us, length us, event | category | flops | bytes accessed | tf_op | source)
XLA Modules:
  0.0 54.3 jit_solution(17999923055333600715)
XLA Ops:
  0.6 51.7 %shard_map.76 = (bf16[32,8192]{1,0:T(8,128)(2,1)}, bf16[4,16,1024]{2,1,0:T(8,128)(2,1)}, bf16[4,16,1024]{2,1,0:T(8,128)(2,1)}) custom-call(bf16[32,8192]{1,0:T(8,128)(2,1)} %q_in.1, bf16[32,1024]{1,0:T(8,128)(2,1)} %k_in.1, bf16[32,1024]{1,0:T(8,128)(2,1)} %v_in.1, s32[64]{0:T(128)} %owner.1, s32[64]{0:T(128)} %slot.1), custom_call_target="tpu_custom_call" | custom-call | tf_op jit(solution)/shard_map/pallas_call | solution.py:451
  52.3 2.0 %shard_map.77 = (bf16[32,8192]{1,0:T(8,128)(2,1)}, bf16[4,16,1024]{2,1,0:T(8,128)(2,1)}, bf16[4,16,1024]{2,1,0:T(8,128)(2,1)}) custom-call(bf16[32,8192]{1,0:T(8,128)(2,1)} %get-tuple-element.6.att, bf16[4,16,1024]{2,1,0:T(8,128)(2,1)} %get-tuple-element.7.key_cache, bf16[4,16,1024]{2,1,0:T(8,128)(2,1)} %get-tuple-element.8.value_cache), custom_call_target="tpu_custom_call" | custom-call | tf_op jit(solution)/shard_map/pallas_call | solution.py:493

commit v4 on v3

--- a/solution.py
+++ b/solution.py
@@ -91,15 +91,10 @@
     sends = []
     for i in (6, 5, 7, 2, 4, 1, 3):
         to, their_side, their_y = partner(i)
-        for which in range(2):
-            src = kv_here.at[which, :, cols((their_y * 2 + their_side) * 128, 128)]
-            sends.append(
-                remote(src, kv_land.at[which, side, y], to, kv_send.at[which, i], kv_recv)
-            )
-            sends[-1].start()
-    for which in range(2):
-        src = kv_here.at[which, :, cols(head * 128, 128)]
-        local(src, kv_land.at[which, side, y], kv_recv).start()
+        src = kv_here.at[:, :, cols((their_y * 2 + their_side) * 128, 128)]
+        sends.append(remote(src, kv_land.at[:, side, y], to, kv_send.at[i], kv_recv))
+        sends[-1].start()
+    local(kv_here.at[:, :, cols(head * 128, 128)], kv_land.at[:, side, y], kv_recv).start()
     for half in range(2):
         src = q_here.at[:, cols(head * 1024 + half * HALF, HALF)]
         local(src, q_land.at[half, side, y], q_recv.at[half]).start()
@@ -114,11 +109,8 @@
     sends[-1].start()
 
     def z_copy(role, way, step):
-        if way == 0:
-            src, dst = lax.rem(8 - step, 8), 7 - step
-        else:
-            src, dst = step, step + 1
-        pick = (role, pl.ds(way * 128, 128)) if isinstance(step, int) and step == 3 else (role,)
+        src, dst = ((8 - step) % 8, 7 - step) if way == 0 else (step, step + 1)
+        pick = (role,) if step < 3 else (role, pl.ds(way * 128, 128))
         return remote(
             kv.at[(src, c) + pick], kv.at[(dst, c) + pick], z_ways[way],
             z_send.at[role, way, step], z_recv.at[role, way, step],
@@ -140,27 +132,19 @@
         return pl.when(pair == which)
 
     def take(role, d):
-        for way, dz in ((0, 8 - d), (1, d)):
-            z_copy(role, way, d - 1).wait_recv()
-
-            @pl.when(d < 3)
-            def _():
+        if d < 4:
+            for way, dz in ((0, 8 - d), (1, d)):
+                z_copy(role, way, d - 1).wait_recv()
                 z_copy(role, way, d).start()
-
-            @pl.when(d == 3)
-            def _():
-                z_copy(role, way, 3).start()
-
+                if role == 0:
+                    cross(dz).start()
+                to_sibling(role, dz).start()
+        else:
+            z_copy(role, 0, 3).wait_recv()
+            z_copy(role, 1, 3).wait_recv()
             if role == 0:
-                cross(dz).start()
-            to_sibling(role, dz).start()
-
-    def take_last(role):
-        z_copy(role, 0, 3).wait_recv()
-        z_copy(role, 1, 3).wait_recv()
-        if role == 0:
-            cross(4).start()
-        to_sibling(role, 4).start()
+                cross(4).start()
+            to_sibling(role, 4).start()
 
     def crossed(dzs):
         for dz in dzs:
@@ -333,36 +317,33 @@
         heard((3,), (0,))
 
     other_units(halves[0], (0,))
+
+    @on_pair(0)
+    def _():
+        take(2, 1)
+
     arrived(q_land.at[1], q_recv.at[1])
     own_units(halves[1], (0,), "diagonal")
     other_units(halves[1], (0,))
 
-    def stage(d, carry):
+    for d in range(1, 4):
         both = (8 - d, d)
-
-        @on_pair(0)
-        def _():
-            take(2, d)
-
+        take(0, d + 1)
+        crossed(both)
         heard((0, 1), both)
         own_units(everything, both, "earlier")
-        crossed(both)
-
-        @pl.when(d < 3)
-        def _():
-            take(0, d + 1)
-            take(1, d + 1)
-
-        @pl.when(d == 3)
-        def _():
-            take_last(0)
-            take_last(1)
+        take(1, d + 1)
+
+        @on_pair(0)
+        def _():
+            take(2, d + 1)
+
+        if d == 3:
             arrived(codes.at[1], t_recv)
             place_pages()
             for which in range(2):
                 for i in range(GROUP):
                     page_copy(i, which).start()
-
         heard((2,), both)
 
         @on_pair(0)
@@ -370,30 +351,35 @@
             heard((3,), both)
 
         other_units(everything, both)
-        return carry
-
-    lax.fori_loop(1, 4, stage, 0)
+
+    crossed((4,))
+    heard((0, 1), (4,))
+    for half in range(2):
+        own_units(halves[half], (4,), "earlier")
 
     @on_pair(0)
     def _():
-        take_last(2)
-
-    heard((0, 1), (4,))
-    own_units(halves[0], (4,), "earlier")
-    crossed((4,))
-    own_units(halves[1], (4,), "earlier")
+        for half in range(2):
+            finish(0, half)
+            send_finished(0, half)
+
     heard((2,), (4,))
 
     @on_pair(0)
     def _():
         heard((3,), (4,))
-
-    for half in range(2):
-        other_units(halves[half], (4,))
-        for which in range(2):
-            finish(which, half)
-        for which in range(2):
-            send_finished(which, half)
+        for half in range(2):
+            attend(1, halves[half], [(2, (4,), "all"), (3, (4,), "all")])
+            finish(1, half)
+            send_finished(1, half)
+
+    @on_pair(1)
+    def _():
+        for which in (1, 0):
+            for half in range(2):
+                attend(which, halves[half], [(2, (4,), "all")])
+                finish(which, half)
+                send_finished(which, half)
 
     for copy in sends:
         copy.wait_send()
@@ -438,10 +424,20 @@
     arrived(att, o_recv)
 
 
-def move(att, key_cache, value_cache, att_out, key_out, value_out):
-    att_out[...] = att[...]
-    key_out[...] = key_cache[...]
-    value_out[...] = value_cache[...]
+def move(att, key_cache, value_cache, att_out, key_out, value_out, held, held_key, held_value, sem):
+    parts = [(key_cache, held_key, key_out), (value_cache, held_value, value_out)]
+    for n in range(4):
+        columns = pl.ds(n * 2048, 2048)
+        parts.append((att.at[:, columns], held.at[:, columns], att_out.at[:, columns]))
+    loads = [pltpu.make_async_copy(src, at, sem.at[0, n]) for n, (src, at, _) in enumerate(parts)]
+    stores = [pltpu.make_async_copy(at, dst, sem.at[1, n]) for n, (_, at, dst) in enumerate(parts)]
+    for load in loads:
+        load.start()
+    for load, store in zip(loads, stores):
+        load.wait()
+        store.start()
+    for store in stores:
+        store.wait()
 
 
 def shards(queries, key_rows, value_rows, page_owner, page_slot):
@@ -469,7 +465,7 @@
             pltpu.VMEM((2, 2, 16, 16, HEAD_DIM), bf16),
             pltpu.VMEM((2, 8, 128), jnp.int32),
             dma((3,)),
-            dma((2, GROUP)),
+            dma((GROUP,)),
             dma,
             dma,
             dma,
@@ -493,8 +489,9 @@
     return pl.pallas_call(
         move,
         out_shape=tuple(jax.ShapeDtypeStruct(a.shape, bf16) for a in held),
-        in_specs=[pl.BlockSpec(memory_space=pltpu.VMEM)] * 3,
-        out_specs=(pl.BlockSpec(memory_space=pltpu.VMEM),) * 3,
+        in_specs=[anywhere] * 3,
+        out_specs=(anywhere,) * 3,
+        scratch_shapes=[pltpu.VMEM(a.shape, bf16) for a in held] + [dma((2, 6))],
     )(*held)
 
 

time: 54.5 us -> 53.2 us (0.976)
  the two profiles are of different devices: /device:TPU:1 before, /device:TPU:2 now
where the time goes in v4:
time: 53.2 us; the launch traced here: 53.1 us
  Pallas kernels  52.3 us (98%)
  between operations  0.8 us (2%)
    pallas_call x1, Pallas kernels, shards(): pl.pallas_call(kernel, out_shape=(jax.ShapeDtypeStruct(queries.shape, bf1...  50.3 us
    pallas_call x1, Pallas kernels, shards(): pl.pallas_call(move, out_shape=tuple((jax.ShapeDtypeStruct(a.shape, bf16)...  1.97 us

profile of v4, /device:TPU:2, one launch (start us, length us, event | category | flops | bytes accessed | tf_op | source)
XLA Modules:
  0.0 53.1 jit_solution(13443389305011196077)
XLA Ops:
  0.6 50.3 %shard_map.76 = (bf16[32,8192]{1,0:T(8,128)(2,1)}, bf16[4,16,1024]{2,1,0:T(8,128)(2,1)}, bf16[4,16,1024]{2,1,0:T(8,128)(2,1)}) custom-call(bf16[32,8192]{1,0:T(8,128)(2,1)} %q_in.1, bf16[32,1024]{1,0:T(8,128)(2,1)} %k_in.1, bf16[32,1024]{1,0:T(8,128)(2,1)} %v_in.1, s32[64]{0:T(128)} %owner.1, s32[64]{0:T(128)} %slot.1), custom_call_target="tpu_custom_call" | custom-call | tf_op jit(solution)/shard_map/pallas_call | solution.py:447
  51.0 2.0 %shard_map.77 = (bf16[32,8192]{1,0:T(8,128)(2,1)}, bf16[4,16,1024]{2,1,0:T(8,128)(2,1)}, bf16[4,16,1024]{2,1,0:T(8,128)(2,1)}) custom-call(bf16[32,8192]{1,0:T(8,128)(2,1)} %get-tuple-element.6.att, bf16[4,16,1024]{2,1,0:T(8,128)(2,1)} %get-tuple-element.7.key_cache, bf16[4,16,1024]{2,1,0:T(8,128)(2,1)} %get-tuple-element.8.value_cache), custom_call_target="tpu_custom_call" | custom-call | tf_op jit(solution)/shard_map/pallas_call | solution.py:489

commit v5 on v4

--- a/solution.py
+++ b/solution.py
@@ -231,8 +231,20 @@
         acc[which, :, spot] = total
 
     def own_units(heads, dzs, kind):
-        attend(1, heads, [(0, dzs, "all"), (1, dzs, kind)])
-        attend(0, heads, [(0, dzs, kind)])
+        if kind == "diagonal":
+            attend(1, heads, [(0, dzs, "all"), (1, dzs, kind)])
+            attend(0, heads, [(0, dzs, kind)])
+            return
+        some = z + max(dzs) >= 8
+
+        @pl.when(some)
+        def _():
+            attend(1, heads, [(0, dzs, "all"), (1, dzs, kind)])
+            attend(0, heads, [(0, dzs, kind)])
+
+        @pl.when(jnp.logical_not(some))
+        def _():
+            attend(1, heads, [(0, dzs, "all")])
 
     def other_units(heads, dzs):
         @on_pair(0)

time: 53.2 us -> 52.4 us (0.985)
  Pallas kernels: 52.3 us -> 51.5 us
    pallas_call x1, Pallas kernels: 50.3 us -> 49.5 us  [shards(): pl.pallas_call(kernel, out_shape=(jax.ShapeDtypeStruct(queries.shape, bf1...]
where the time goes in v5:
time: 52.4 us; the launch traced here: 52.3 us
  Pallas kernels  51.5 us (98%)
  between operations  0.82 us (2%)
    pallas_call x1, Pallas kernels, shards(): pl.pallas_call(kernel, out_shape=(jax.ShapeDtypeStruct(queries.shape, bf1...  49.5 us
    pallas_call x1, Pallas kernels, shards(): pl.pallas_call(move, out_shape=tuple((jax.ShapeDtypeStruct(a.shape, bf16)...  1.97 us

profile of v5, /device:TPU:2, one launch (start us, length us, event | category | flops | bytes accessed | tf_op | source)
XLA Modules:
  0.0 52.3 jit_solution(7689889801311272664)
XLA Ops:
  0.6 49.5 %shard_map.76 = (bf16[32,8192]{1,0:T(8,128)(2,1)}, bf16[4,16,1024]{2,1,0:T(8,128)(2,1)}, bf16[4,16,1024]{2,1,0:T(8,128)(2,1)}) custom-call(bf16[32,8192]{1,0:T(8,128)(2,1)} %q_in.1, bf16[32,1024]{1,0:T(8,128)(2,1)} %k_in.1, bf16[32,1024]{1,0:T(8,128)(2,1)} %v_in.1, s32[64]{0:T(128)} %owner.1, s32[64]{0:T(128)} %slot.1), custom_call_target="tpu_custom_call" | custom-call | tf_op jit(solution)/shard_map/pallas_call | solution.py:459
  50.2 2.0 %shard_map.77 = (bf16[32,8192]{1,0:T(8,128)(2,1)}, bf16[4,16,1024]{2,1,0:T(8,128)(2,1)}, bf16[4,16,1024]{2,1,0:T(8,128)(2,1)}) custom-call(bf16[32,8192]{1,0:T(8,128)(2,1)} %get-tuple-element.6.att, bf16[4,16,1024]{2,1,0:T(8,128)(2,1)} %get-tuple-element.7.key_cache, bf16[4,16,1024]{2,1,0:T(8,128)(2,1)} %get-tuple-element.8.value_cache), custom_call_target="tpu_custom_call" | custom-call | tf_op jit(solution)/shard_map/pallas_call | solution.py:501

commit v6 on v5

--- a/solution.py
+++ b/solution.py
@@ -235,12 +235,19 @@
             attend(1, heads, [(0, dzs, "all"), (1, dzs, kind)])
             attend(0, heads, [(0, dzs, kind)])
             return
-        some = z + max(dzs) >= 8
-
-        @pl.when(some)
-        def _():
-            attend(1, heads, [(0, dzs, "all"), (1, dzs, kind)])
-            attend(0, heads, [(0, dzs, kind)])
+        every, some = z + min(dzs) >= 8, z + max(dzs) >= 8
+
+        @pl.when(every)
+        def _():
+            attend(1, heads, [(0, dzs, "all"), (1, dzs, "all")])
+            attend(0, heads, [(0, dzs, "all")])
+
+        if len(dzs) > 1:
+
+            @pl.when(some & jnp.logical_not(every))
+            def _():
+                attend(1, heads, [(0, dzs, "all"), (1, (max(dzs),), "all")])
+                attend(0, heads, [(0, (max(dzs),), "all")])
 
         @pl.when(jnp.logical_not(some))
         def _():

time: 52.4 us -> 52.4 us (level)
  no operation moved by 1% of the time
where the time goes in v6:
time: 52.4 us; the launch traced here: 52.3 us
  Pallas kernels  51.4 us (98%)
  between operations  0.82 us (2%)
    pallas_call x1, Pallas kernels, shards(): pl.pallas_call(kernel, out_shape=(jax.ShapeDtypeStruct(queries.shape, bf1...  49.5 us
    pallas_call x1, Pallas kernels, shards(): pl.pallas_call(move, out_shape=tuple((jax.ShapeDtypeStruct(a.shape, bf16)...  1.97 us

profile of v6, /device:TPU:2, one launch (start us, length us, event | category | flops | bytes accessed | tf_op | source)
XLA Modules:
  0.0 52.3 jit_solution(11414236366830354515)
XLA Ops:
  0.6 49.5 %shard_map.76 = (bf16[32,8192]{1,0:T(8,128)(2,1)}, bf16[4,16,1024]{2,1,0:T(8,128)(2,1)}, bf16[4,16,1024]{2,1,0:T(8,128)(2,1)}) custom-call(bf16[32,8192]{1,0:T(8,128)(2,1)} %q_in.1, bf16[32,1024]{1,0:T(8,128)(2,1)} %k_in.1, bf16[32,1024]{1,0:T(8,128)(2,1)} %v_in.1, s32[64]{0:T(128)} %owner.1, s32[64]{0:T(128)} %slot.1), custom_call_target="tpu_custom_call" | custom-call | tf_op jit(solution)/shard_map/pallas_call | solution.py:466
  50.1 2.0 %shard_map.77 = (bf16[32,8192]{1,0:T(8,128)(2,1)}, bf16[4,16,1024]{2,1,0:T(8,128)(2,1)}, bf16[4,16,1024]{2,1,0:T(8,128)(2,1)}) custom-call(bf16[32,8192]{1,0:T(8,128)(2,1)} %get-tuple-element.6.att, bf16[4,16,1024]{2,1,0:T(8,128)(2,1)} %get-tuple-element.7.key_cache, bf16[4,16,1024]{2,1,0:T(8,128)(2,1)} %get-tuple-element.8.value_cache), custom_call_target="tpu_custom_call" | custom-call | tf_op jit(solution)/shard_map/pallas_call | solution.py:508
